TPU v7x, 32 devices: a whole 2x2x4 slice. The times are simulated.
32 devices in a mesh: row: 8 (over z, core), col: 4 (over y, x).
Axes of the slice: x: 2, y: 2, z: 4, core: 2. Of those that a mesh axis runs over, the one named last changes fastest.
Arguments:
- factor: bfloat16 [28672, 28672], P('row', 'col'), may hold values from -8 to 50
- subspace: bfloat16 [28672, 1024], P(('col', 'row')), may hold values from -6 to 6
Outputs:
- new_basis: float32 [28672, 1024], P(('row', 'col'))
- r_factor: float32 [1024, 1024], replicated
All inputs are finite; a program needn't handle non-finite values.
Results may differ from a plain program's by a relative error of at most 0.0009.
Values may be sent and summed in bfloat16 or wider, within the bound.
No kernel may reach another device: no remote copies, remote signals or barrier semaphores. Data moves between devices by JAX's collectives and lax.ppermute only.
A program may use at most 192 MiB of HBM per device.

v0:
```python
import jax
import jax.numpy as jnp
from jax import lax
from jax.sharding import PartitionSpec as P

N = 28672


def body(factor, subspace):
    partial_panel = jnp.dot(
        factor,
        lax.all_gather(subspace, "row", axis=0, tiled=True),
        preferred_element_type=jnp.float32,
    )
    image_panel = lax.psum_scatter(partial_panel, "col", scatter_dimension=0, tiled=True)
    local_gram = lax.dot_general(
        image_panel,
        image_panel,
        (((0,), (0,)), ((), ())),
        precision=lax.Precision.HIGHEST,
        preferred_element_type=jnp.float32,
    )
    gram_total = lax.psum(local_gram, ("row", "col"))
    gram_matrix = gram_total / N
    symmetric = (gram_matrix + gram_matrix.T) / 2.0
    lower_factor = jnp.linalg.cholesky(symmetric)
    solved = lax.linalg.triangular_solve(lower_factor, image_panel.T, left_side=True, lower=True)
    return (solved.T, lower_factor.T)


def solution(mesh):
    placed = (P("row", "col"), P(("col", "row"), None))
    return jax.shard_map(
        body, mesh=mesh, in_specs=placed, out_specs=(P(("row", "col"), None), P()), check_vma=False
    )
```

profile of v0, /device:TPU:1, one launch (start us, length us, event | category | flops | bytes accessed | tf_op | source)
XLA Modules:
  0.0 902.4 jit_solution(3071609483294074169)
XLA Ops:
  7.9 138.2 %all-gather.2.cloned.1.call-done = bf16[7168,1024]{1,0:T(8,128)(2,1)} async-done(((bf16[896,1024]{1,0:T(8,128)(2,1)}), bf16[7168,1024]{1,0:T(8,128)(2,1)}) %all-gather.2.cloned.1.call-update) | async-done | bytes 14680080 | tf_op jit(solution)/shard_map/all_gather | solution.py:12
  146.1 62.7 %fusion.73 = f32[3584,1024]{1,0:T(8,128)} fusion(bf16[3584,7168]{1,0:T(8,128)(2,1)} %param.2, bf16[7168,1024]{1,0:T(8,128)(2,1)} %all-gather.2.cloned.1.call-done), kind=kOutput, calls=%fused_computation.162 | convolution fusion | flops 52613349376 | bytes 80740352 | tf_op jit(solution)/shard_map/dot_general | solution.py:10
  209.2 135.5 %reduce-scatter.2.cloned.1.call-done = f32[896,1024]{1,0:T(8,128)} async-done(((f32[3584,1024]{1,0:T(8,128)}), f32[896,1024]{1,0:T(8,128)}) %reduce-scatter.2.cloned.1.call-update) | async-done | bytes 3670032 | tf_op jit(solution)/shard_map/reduce_scatter | solution.py:15
  344.7 17.5 %fusion.74 = f32[1024,1024]{0,1:T(8,128)} fusion(f32[896,1024]{1,0:T(8,128)} %reduce-scatter.2.cloned.1.call-done), kind=kOutput, calls=%fused_computation.163 | convolution fusion | flops 11274289152 | bytes 7864320 | tf_op jit(solution)/shard_map/dot_general | solution.py:16
  362.3 140.0 %all-reduce.3.cloned.1.call-done = f32[1024,1024]{0,1:T(8,128)} async-done(((f32[1024,1024]{0,1:T(8,128)}), f32[1024,1024]{0,1:T(8,128)}) %all-reduce.3.cloned.1.call-update) | async-done | bytes 4194320 | tf_op jit(solution)/shard_map/psum | solution.py:23
  502.3 5.1 broadcast_multiply_fusion
  507.4 5.3 copy.5
  512.8 6.9 fusion.1
  519.7 5.8 copy.6
  525.6 4.4 fusion
  530.0 1.9 copy-done
  532.0 11.7 %cholesky.223 = f32[128,128]{1,0:T(8,128)S(1)} custom-call(f32[128,128]{1,0:T(8,128)S(1)} %cholesky.580), custom_call_target="Cholesky" | custom-call | tf_op jit(solution)/shard_map/jit(cholesky)/cholesky | solution.py:26
  543.7 9.8 %custom-call.62 = f32[1,128,128]{1,2,0:T(8,128)S(1)} custom-call(f32[1,128,128]{2,1,0:T(8,128)S(1)} %get-tuple-element.70), custom_call_target="InvertDiagBlocksLowerTriangular" | custom-call | tf_op jit(solution)/shard_map/jit(cholesky)/cholesky | solution.py:26
  553.5 2.5 cholesky.255
  556.1 2.3 constant_dynamic-update-slice_fusion.32
  558.4 1.5 convolution_subtract_fusion.5
  559.9 11.9 %cholesky.244 = f32[128,128]{1,0:T(8,128)S(1)} custom-call(f32[128,128]{1,0:T(8,128)S(1)} %cholesky.584), custom_call_target="Cholesky" | custom-call | tf_op jit(solution)/shard_map/jit(cholesky)/cholesky | solution.py:26
  572.4 9.8 %custom-call.63 = f32[1,128,128]{1,2,0:T(8,128)S(1)} custom-call(f32[1,128,128]{2,1,0:T(8,128)S(1)} %get-tuple-element.67), custom_call_target="InvertDiagBlocksLowerTriangular" | custom-call | tf_op jit(solution)/shard_map/jit(cholesky)/cholesky | solution.py:26
  582.2 1.2 convolution_dynamic-update-slice_fusion.1
  583.5 2.1 convolution_subtract_fusion.6
  585.6 11.7 %cholesky.468 = f32[128,128]{1,0:T(8,128)S(1)} custom-call(f32[128,128]{1,0:T(8,128)S(1)} %cholesky.589), custom_call_target="Cholesky" | custom-call | tf_op jit(solution)/shard_map/jit(cholesky)/cholesky | solution.py:26
  598.6 9.8 %custom-call.64 = f32[1,128,128]{1,2,0:T(8,128)S(1)} custom-call(f32[1,128,128]{2,1,0:T(8,128)S(1)} %get-tuple-element.64), custom_call_target="InvertDiagBlocksLowerTriangular" | custom-call | tf_op jit(solution)/shard_map/jit(cholesky)/cholesky | solution.py:26
  609.5 2.3 convolution_subtract_fusion.7
  611.9 11.9 %cholesky.487 = f32[128,128]{1,0:T(8,128)S(1)} custom-call(f32[128,128]{1,0:T(8,128)S(1)} %cholesky.594), custom_call_target="Cholesky" | custom-call | tf_op jit(solution)/shard_map/jit(cholesky)/cholesky | solution.py:26
  625.1 9.8 %custom-call.65 = f32[1,128,128]{1,2,0:T(8,128)S(1)} custom-call(f32[1,128,128]{2,1,0:T(8,128)S(1)} %get-tuple-element.61), custom_call_target="InvertDiagBlocksLowerTriangular" | custom-call | tf_op jit(solution)/shard_map/jit(cholesky)/cholesky | solution.py:26
  636.0 2.3 convolution_subtract_fusion.8
  638.3 11.7 %cholesky.506 = f32[128,128]{1,0:T(8,128)S(1)} custom-call(f32[128,128]{1,0:T(8,128)S(1)} %cholesky.599), custom_call_target="Cholesky" | custom-call | tf_op jit(solution)/shard_map/jit(cholesky)/cholesky | solution.py:26
  651.4 10.2 %custom-call.66 = f32[1,128,128]{1,2,0:T(8,128)S(1)} custom-call(f32[1,128,128]{2,1,0:T(8,128)S(1)} %get-tuple-element.58), custom_call_target="InvertDiagBlocksLowerTriangular" | custom-call | tf_op jit(solution)/shard_map/jit(cholesky)/cholesky | solution.py:26
  662.6 2.3 convolution_subtract_fusion.9
  664.9 11.7 %cholesky.526 = f32[128,128]{1,0:T(8,128)S(1)} custom-call(f32[128,128]{1,0:T(8,128)S(1)} %cholesky.604), custom_call_target="Cholesky" | custom-call | tf_op jit(solution)/shard_map/jit(cholesky)/cholesky | solution.py:26
  677.9 9.8 %custom-call.67 = f32[1,128,128]{1,2,0:T(8,128)S(1)} custom-call(f32[1,128,128]{2,1,0:T(8,128)S(1)} %get-tuple-element.55), custom_call_target="InvertDiagBlocksLowerTriangular" | custom-call | tf_op jit(solution)/shard_map/jit(cholesky)/cholesky | solution.py:26
  688.6 2.1 convolution_subtract_fusion.10
  690.7 11.9 %cholesky.546 = f32[128,128]{1,0:T(8,128)S(1)} custom-call(f32[128,128]{1,0:T(8,128)S(1)} %cholesky.609), custom_call_target="Cholesky" | custom-call | tf_op jit(solution)/shard_map/jit(cholesky)/cholesky | solution.py:26
  703.9 9.8 %custom-call.68 = f32[1,128,128]{1,2,0:T(8,128)S(1)} custom-call(f32[1,128,128]{2,1,0:T(8,128)S(1)} %get-tuple-element.52), custom_call_target="InvertDiagBlocksLowerTriangular" | custom-call | tf_op jit(solution)/shard_map/jit(cholesky)/cholesky | solution.py:26
  714.5 1.8 convolution_subtract_fusion.11
  716.3 11.7 %cholesky.564 = f32[128,128]{1,0:T(8,128)S(1)} custom-call(f32[128,128]{1,0:T(8,128)S(1)} %convolution_subtract_fusion.11), custom_call_target="Cholesky" | custom-call | tf_op jit(solution)/shard_map/jit(cholesky)/cholesky | solution.py:26
  735.0 6.6 fusion.3
  741.6 5.3 copy.8
  746.9 22.8 %while.1 = (s32[]{:T(128)}, f32[1024,1024]{1,0:T(8,128)}, s32[8,2]{0,1:T(2,128)S(1)}, f32[8,128,128]{2,1,0:T(8,128)S(1)}, s32[]{:T(128)}) while((s32[]{:T(128)}, f32[1024,1024]{1,0:T(8,128)}, s32[8,2]{0,1:T(2,128)S(1)}, f32[8,128,128]{2,1,0:T(8,128)S(1)}, s32[]{:T(128)}) %tuple.63), condition=%wide.while_cond, body=%wide.while_body.sunk | while | flops 2 | bytes 131189 | solution.py:27
  747.5 2.2 bitcast_dynamic-update-slice_fusion.2
  750.4 2.2 bitcast_dynamic-update-slice_fusion.2
  753.3 2.2 bitcast_dynamic-update-slice_fusion.2
  756.1 2.2 bitcast_dynamic-update-slice_fusion.2
  759.0 2.2 bitcast_dynamic-update-slice_fusion.2
  761.8 2.2 bitcast_dynamic-update-slice_fusion.2
  764.7 2.2 bitcast_dynamic-update-slice_fusion.2
  767.6 2.2 bitcast_dynamic-update-slice_fusion.2
  769.7 78.8 %custom-call.69 = f32[8,128,128]{1,2,0:T(8,128)S(1)} custom-call(f32[8,128,128]{2,1,0:T(8,128)S(1)} %get-tuple-element.9), custom_call_target="InvertDiagBlocksLowerTriangular" | custom-call | tf_op jit(solution)/shard_map/triangular_solve | solution.py:27
  848.6 2.7 constant_dynamic-update-slice_fusion.17
  851.2 2.0 convolution_subtract_fusion.4
  853.2 1.5 constant_dynamic-update-slice_fusion.16
  854.7 2.5 convolution_subtract_fusion.2
  857.2 1.5 constant_dynamic-update-slice_fusion.15
  858.7 3.4 fusion.18
  862.1 1.5 constant_dynamic-update-slice_fusion.14
  863.6 4.0 fusion.21
  867.7 1.4 constant_dynamic-update-slice_fusion.13
  869.1 5.3 convolution_subtract_fusion.3
  874.4 1.4 constant_dynamic-update-slice_fusion.12
  875.9 5.5 convolution_subtract_fusion.1
  881.4 1.4 constant_dynamic-update-slice_fusion.11
  882.8 6.5 convolution_subtract_fusion
  889.3 1.4 convolution_dynamic-update-slice_fusion
  890.7 5.0 copy.7
  (55 shorter events, 20.3 us)
Async XLA Ops:
  7.2 138.9 %all-gather.2.cloned.1.call-start = ((), (), s32[]{:S(2)}) async-start(), calls=%async_computation.1 | async-start | bytes 16515072 | tf_op jit(solution)/shard_map/all_gather | solution.py:12
  7.9 336.8 %reduce-scatter.2.cloned.1.call-start = ((), (), s32[]{:S(2)}) async-start(), calls=%async_computation.2 | async-start | bytes 18350080 | tf_op jit(solution)/shard_map/reduce_scatter | solution.py:15
  208.9 293.4 %all-reduce.3.cloned.1.call-start = ((), (), s32[]{:S(2)}) async-start(), calls=%async_computation.3 | async-start | bytes 8388608 | tf_op jit(solution)/shard_map/psum | solution.py:23
  530.0 1.9 copy-start
  848.6 6.1 copy-start.1
Sparse Core Ops, SparseCore 0:
  9.6 136.4 all-gather.1
  209.0 135.7 reduce-scatter.1
  362.4 139.8 all-reduce.2
where the time goes:
time: 911 us; the launch traced here: 902 us
  waiting for transfers between devices  414 us (45%)
  other arithmetic  274 us (30%)
  matrix products  145 us (16%)
  local copies, waits for them, and re-layouts  48.7 us (5%)
  between operations  19.1 us (2%)
    another operation x30, other arithmetic, body(): lower_factor = jnp.linalg.cholesky(symmetric)  172 us
    psum x1, waiting for transfers between devices, body(): gram_total = lax.psum(local_gram, ('row', 'col'))  140 us
    all_gather x1, waiting for transfers between devices, body(): lax.all_gather(subspace, 'row', axis=0, tiled=True)  138 us
    reduce_scatter x1, waiting for transfers between devices, body(): lax.psum_scatter(partial_panel, 'col', scatter_dimension=0, tiled=True)  136 us
    another operation x2, other arithmetic, body(): lax.linalg.triangular_solve(lower_factor, image_panel.T, left_side=True,...  78.8 us
    dot_general x1, matrix products, body(): jnp.dot(factor, lax.all_gather(subspace, 'row', axis=0, tiled=True), pref...  62.7 us
    another operation x15, matrix products, body(): lax.linalg.triangular_solve(lower_factor, image_panel.T, left_side=True,...  42.1 us
    another operation x14, matrix products, body(): lower_factor = jnp.linalg.cholesky(symmetric)  23 us
  transfers between devices with their start and end apart: 3, of which 3 were waited for; matrix products, arithmetic and copies ran while one was open for 0% of the time, Pallas kernels for 0%

commit v1 on v0

v1 whole, which is shorter than its diff:
```python
import functools

import jax
import jax.numpy as jnp
from jax import lax
from jax.experimental import pallas as pl
from jax.experimental.pallas import tpu as pltpu
from jax.sharding import PartitionSpec as P

WIDTHS = (256, 256, 256, 256)
PIVOTS = 128
TILE = 8
HIGHEST = lax.Precision.HIGHEST


def gather_rows(block, cores, size):
    levels = size // cores
    index = lax.axis_index("row")
    level, core = index // cores, index % cores
    rows = block.shape[0]
    swap = [(i, i ^ 1) for i in range(size)]
    up = [(i, i + cores) for i in range(size - cores)]
    down = [(i + cores, i) for i in range(size - cores)]

    rising, falling = [block], [block]
    for _ in range(levels - 1):
        rising.append(lax.ppermute(rising[-1], "row", up))
        falling.append(lax.ppermute(falling[-1], "row", down))
    panel = jnp.zeros((size, rows, block.shape[1]), block.dtype)

    def put(panel, piece, slot):
        return lax.dynamic_update_slice(panel, piece[None], (slot, 0, 0))

    other = [lax.ppermute(block, "row", swap)]
    panel = put(panel, block, index)
    panel = put(panel, other[0], level * cores + 1 - core)
    rising_other = [None] + [lax.ppermute(p, "row", swap) for p in rising[1:]]
    falling_other = [None] + [lax.ppermute(p, "row", swap) for p in falling[1:]]
    for step in range(1, levels):
        slot = (level - step + levels) % levels * cores
        from_below = level >= step
        mine = jnp.where(from_below, rising[step], falling[levels - step])
        theirs = jnp.where(from_below, rising_other[step], falling_other[levels - step])
        panel = put(panel, mine, slot + core)
        panel = put(panel, theirs, slot + 1 - core)
    return panel.reshape(size * rows, block.shape[1])


def exchange_columns(partial, size):
    rows = partial.shape[0] // size
    width = partial.shape[1]
    index = lax.axis_index("col")
    pieces = partial.reshape(size, rows, width)
    top = jnp.max(jnp.abs(pieces), axis=1)
    exponent = jnp.ceil(jnp.log2(jnp.maximum(top, 1e-30)))
    total = lax.dynamic_index_in_dim(pieces, index, 0, keepdims=False)
    for step in range(1, size):
        to = (index + step) % size
        piece = lax.dynamic_index_in_dim(pieces, to, 0, keepdims=False)
        power = lax.dynamic_index_in_dim(exponent, to, 0, keepdims=True)
        coded = (piece * jnp.exp2(14.0 - power)).astype(jnp.float16)
        tail = jnp.broadcast_to(power, (16, width)).astype(jnp.float16)
        sent = jnp.concatenate([coded, tail], axis=0)
        got = lax.ppermute(sent, "col", [(i, (i + step) % size) for i in range(size)])
        got = got.astype(jnp.float32)
        total = total + got[:rows] * jnp.exp2(got[rows : rows + 1] - 14.0)
    return total


def scatter_axis(block, axis, size, index, perm):
    rows = block.shape[0] // size
    total = lax.dynamic_slice_in_dim(block, index * rows, rows, 0)
    for step in range(1, size):
        piece = lax.dynamic_slice_in_dim(block, (index + step) % size * rows, rows, 0)
        total = total + lax.ppermute(piece, axis, perm(step))
    return total


def gather_axis(block, axis, size, index, perm):
    rows = block.shape[0]
    whole = jnp.zeros((size * rows, block.shape[1]), block.dtype)
    whole = lax.dynamic_update_slice_in_dim(whole, block, index * rows, 0)
    for step in range(1, size):
        got = lax.ppermute(block, axis, perm(step))
        whole = lax.dynamic_update_slice_in_dim(whole, got, (index - step + size) % size * rows, 0)
    return whole


def sum_everywhere(block, cores, row_size, col_size):
    levels = row_size // cores
    row = lax.axis_index("row")
    level, core = row // cores, row % cores
    col = lax.axis_index("col")
    core_perm = lambda step: [(i, i // cores * cores + (i + step) % cores) for i in range(row_size)]
    col_perm = lambda step: [(i, (i + step) % col_size) for i in range(col_size)]
    level_perm = lambda step: [(i, (i + step * cores) % row_size) for i in range(row_size)]
    stages = (("row", cores, core, core_perm), ("col", col_size, col, col_perm), ("row", levels, level, level_perm))
    for axis, size, index, perm in stages:
        block = scatter_axis(block, axis, size, index, perm)
    for axis, size, index, perm in reversed(stages):
        block = gather_axis(block, axis, size, index, perm)
    return block


def eliminate(block):
    groups = PIVOTS // TILE
    lane = lax.broadcasted_iota(jnp.int32, (TILE, PIVOTS), 1)
    sub = lax.broadcasted_iota(jnp.int32, (TILE, PIVOTS), 0)
    held = [block[g * TILE : (g + 1) * TILE] for g in range(groups)]
    factor, inverse = [], []
    for g in range(groups):
        for i in range(TILE):
            j = g * TILE + i
            at = lane == j
            row = jnp.broadcast_to(held[g][i : i + 1], (TILE, PIVOTS))
            pivot = jnp.broadcast_to(row[:, j : j + 1], (TILE, PIVOTS))
            scaled = jnp.where(at, 1.0, row) / pivot
            for h in range(g, groups):
                if h == g and i == TILE - 1:
                    continue
                weight = jnp.broadcast_to(held[h][:, j : j + 1], (TILE, PIVOTS))
                new = jnp.where(at, 0.0, held[h]) - weight * scaled
                held[h] = jnp.where(sub > i, new, held[h]) if h == g else new
        own = sub + g * TILE
        diagonal = jnp.sum(jnp.where(lane == own, held[g], 0.0), axis=1, keepdims=True)
        root = lax.rsqrt(diagonal)
        root = root * (1.5 - 0.5 * diagonal * root * root)
        factor.append(jnp.where(lane >= own, held[g] * root, 0.0))
        inverse.append(jnp.where(lane < own, held[g] * root, jnp.where(lane == own, root, 0.0)))
    return jnp.concatenate(factor, 0), jnp.concatenate(inverse, 0)


def mul(a, b):
    return jnp.dot(a, b, precision=HIGHEST, preferred_element_type=jnp.float32)


def column_kernel(scale, before, width, gram_ref, *refs):
    factor_ref, inverse_ref = refs[-2:]
    block = gram_ref[before:, :] * scale
    if before:
        above = mul(refs[0][...], gram_ref[:before, :] * scale)
        factor_ref[:before, :] = above
        above_t = above.T
        block = block - mul(above_t, above)
    block = (block + block.T) * 0.5
    if width == PIVOTS:
        factor, inverse = eliminate(block)
    else:
        first, first_inverse = eliminate(block[:PIVOTS, :PIVOTS])
        corner = mul(first_inverse, block[:PIVOTS, PIVOTS:])
        corner_t = corner.T
        last, last_inverse = eliminate(block[PIVOTS:, PIVOTS:] - mul(corner_t, corner))
        low = -mul(last_inverse, mul(corner_t, first_inverse))
        none = jnp.zeros((PIVOTS, PIVOTS), jnp.float32)
        factor = jnp.concatenate(
            [jnp.concatenate([first, corner], 1), jnp.concatenate([none, last], 1)], 0
        )
        inverse = jnp.concatenate(
            [jnp.concatenate([first_inverse, none], 1), jnp.concatenate([low, last_inverse], 1)], 0
        )
    factor_ref[before:, :] = factor
    inverse_ref[:, before:] = inverse
    if before:
        inverse_ref[:, :before] = -mul(mul(inverse, above_t), refs[0][...])


def factor_column(gram, inverse_before, scale):
    width = gram.shape[1]
    before = gram.shape[0] - width
    operands = (gram,) if inverse_before is None else (gram, inverse_before)
    return pl.pallas_call(
        functools.partial(column_kernel, scale, before, width),
        out_shape=(
            jax.ShapeDtypeStruct((before + width, width), jnp.float32),
            jax.ShapeDtypeStruct((width, before + width), jnp.float32),
        ),
        in_specs=[pl.BlockSpec(memory_space=pltpu.VMEM)] * len(operands),
        out_specs=(pl.BlockSpec(memory_space=pltpu.VMEM),) * 2,
        compiler_params=pltpu.CompilerParams(vmem_limit_bytes=32 * 1024 * 1024),
        cost_estimate=pl.CostEstimate(flops=20_000_000_000, bytes_accessed=4_000_000, transcendentals=0),
    )(*operands)


def body(row_size, col_size, cores, factor, subspace):
    total_rows = factor.shape[1] * col_size
    scale = 1.0 / total_rows
    images, bases, columns = [], [], []
    inverse = None
    start = 0
    for width in WIDTHS:
        with jax.named_scope(f"chunk{start}"):
            panel = gather_rows(lax.slice_in_dim(subspace, start, start + width, axis=1), cores, row_size)
            partial = jnp.dot(factor, panel, preferred_element_type=jnp.float32)
            images.append(exchange_columns(partial, col_size))
            so_far = jnp.concatenate(images, axis=1)
            gram = lax.dot_general(
                so_far, images[-1], (((0,), (0,)), ((), ())), precision=HIGHEST, preferred_element_type=jnp.float32
            )
            gram = sum_everywhere(gram, cores, row_size, col_size)
            column, last_rows = factor_column(gram, inverse, scale)
            bases.append(
                lax.dot_general(
                    so_far, last_rows, (((1,), (1,)), ((), ())), precision=lax.Precision.HIGH, preferred_element_type=jnp.float32
                )
            )
            if inverse is None:
                inverse = last_rows
            else:
                inverse = jnp.concatenate([jnp.pad(inverse, ((0, 0), (0, width))), last_rows], axis=0)
            start += width
            columns.append(jnp.pad(column, ((0, subspace.shape[1] - start), (0, 0))))
    return jnp.concatenate(bases, axis=1), jnp.concatenate(columns, axis=1)


def solution(mesh):
    row_size, col_size = mesh.shape["row"], mesh.shape["col"]
    return jax.shard_map(
        functools.partial(body, row_size, col_size, 2),
        mesh=mesh,
        in_specs=(P("row", "col"), P(("col", "row"), None)),
        out_specs=(P(("row", "col"), None), P()),
        check_vma=False,
    )
```

time: 911 us -> 747 us (0.82)
  waiting for transfers between devices: 414 us -> 171 us
  other arithmetic: 274 us -> 45.2 us
  starting transfers between devices: 0.41 us -> 177 us
  Pallas kernels: 0 us -> 155 us
  matrix products: 145 us -> 110 us
  local copies, waits for them, and re-layouts: 48.7 us -> 77.5 us
  between operations: 19.1 us -> 3 us
    another operation x32 -> x0, other arithmetic: 251 us -> none  [the longest x30 172 us: body(): lower_factor = jnp.linalg.cholesky(symmetric)]
    ppermute x0 -> x120, starting transfers between devices: none -> 177 us  [the longest x28 46.5 us: gather_axis(): got = lax.ppermute(block, axis, perm(step))]
    ppermute x0 -> x120, waiting for transfers between devices: none -> 171 us  [the longest x12 67.3 us: exchange_columns(): lax.ppermute(sent, 'col', [(i, (i + step) % size) for i in range(size)])]
    pallas_call x0 -> x4, Pallas kernels: none -> 155 us  [factor_column(): pl.pallas_call(functools.partial(column_kernel, scale, before, width), ou...]
    psum x1 -> x0, waiting for transfers between devices: 140 us -> none  [body(): gram_total = lax.psum(local_gram, ('row', 'col'))]
    all_gather x1 -> x0, waiting for transfers between devices: 138 us -> none  [body(): lax.all_gather(subspace, 'row', axis=0, tiled=True)]
    reduce_scatter x1 -> x0, waiting for transfers between devices: 136 us -> none  [body(): lax.psum_scatter(partial_panel, 'col', scatter_dimension=0, tiled=True)]
    another operation x29 -> x0, matrix products: 65.1 us -> none  [the longest x15 42.1 us: body(): lax.linalg.triangular_solve(lower_factor, image_panel.T, left_side=True,...]
  transfers between devices with their start and end apart: 3 -> 120, of which waited for: 3 -> 41; matrix products, arithmetic and copies ran while one was open for 0% -> 18% of each run, Pallas kernels for 0% -> 15%
where the time goes in v1:
time: 747 us; the launch traced here: 740 us
  starting transfers between devices  177 us (24%)
  waiting for transfers between devices  171 us (23%)
  Pallas kernels  155 us (21%)
  matrix products  110 us (15%)
  local copies, waits for them, and re-layouts  77.5 us (10%)
  other arithmetic  45.2 us (6%)
    pallas_call x4, Pallas kernels, factor_column(): pl.pallas_call(functools.partial(column_kernel, scale, before, width), ou...  155 us
    dot_general x4, matrix products, body(): partial = jnp.dot(factor, panel, preferred_element_type=jnp.float32)  96.1 us
    ppermute x12, waiting for transfers between devices, exchange_columns(): lax.ppermute(sent, 'col', [(i, (i + step) % size) for i in range(size)])  67.3 us
    ppermute x12, waiting for transfers between devices, gather_rows(): falling.append(lax.ppermute(falling[-1], 'row', down))  63.6 us
    ppermute x28, starting transfers between devices, gather_axis(): got = lax.ppermute(block, axis, perm(step))  46.5 us
    ppermute x12, starting transfers between devices, gather_rows(): rising.append(lax.ppermute(rising[-1], 'row', up))  46.2 us
    ppermute x28, starting transfers between devices, scatter_axis(): total = total + lax.ppermute(piece, axis, perm(step))  37.4 us
    dynamic_slice x4, local copies, waits for them, and re-layouts, exchange_columns(): total = lax.dynamic_index_in_dim(pieces, index, 0, keepdims=False)  29.2 us
  transfers between devices with their start and end apart: 120, of which 41 were waited for; matrix products, arithmetic and copies ran while one was open for 18% of the time, Pallas kernels for 15%

profile of v1, /device:TPU:1, one launch (start us, length us, event | category | flops | bytes accessed | tf_op | source)
XLA Modules:
  0.0 739.7 jit_solution(5076127667442113224)
XLA Ops:
  0.6 2.5 fusion.106
  4.5 6.1 collective-permute-start.31
  33.5 6.1 collective-permute-done.62
  40.9 8.4 %collective-permute-done.33 = bf16[896,256]{1,0:T(8,128)(2,1)S(1)} collective-permute-done((bf16[896,256]{1,0:T(8,128)(2,1)}, bf16[896,256]{1,0:T(8,128)(2,1)S(1)}, u32[]{:S(2)}, u32[]{:S(2)}) %collective-permute-start.33) | collective-permute-done | bytes 458784 | tf_op jit(solution)/shard_map/chunk256/ppermute | solution.py:28
  51.5 4.0 collective-permute-start.1
  55.5 3.8 collective-permute-done.92
  60.6 8.4 %collective-permute-done.3 = bf16[896,256]{1,0:T(8,128)(2,1)S(1)} collective-permute-done((bf16[896,256]{1,0:T(8,128)(2,1)}, bf16[896,256]{1,0:T(8,128)(2,1)S(1)}, u32[]{:S(2)}, u32[]{:S(2)}) %collective-permute-start.3) | collective-permute-done | bytes 458784 | tf_op jit(solution)/shard_map/chunk0/ppermute | solution.py:28
  71.1 7.7 %collective-permute-done.63 = bf16[896,256]{1,0:T(8,128)(2,1)S(1)} collective-permute-done((bf16[896,256]{1,0:T(8,128)(2,1)}, bf16[896,256]{1,0:T(8,128)(2,1)S(1)}, u32[]{:S(2)}, u32[]{:S(2)}) %collective-permute-start.63) | collective-permute-done | bytes 458784 | tf_op jit(solution)/shard_map/chunk512/ppermute | solution.py:28
  78.9 3.2 collective-permute-start.61
  82.0 6.7 collective-permute-done.34
  90.9 5.0 collective-permute-start.91
  95.9 2.6 collective-permute-done.93
  99.3 9.1 %collective-permute-done.4 = bf16[896,256]{1,0:T(8,128)(2,1)S(1)} collective-permute-done((bf16[896,256]{1,0:T(8,128)(2,1)S(1)}, bf16[896,256]{1,0:T(8,128)(2,1)S(1)}, u32[]{:S(2)}, u32[]{:S(2)}) %collective-permute-start.4) | collective-permute-done | bytes 458784 | tf_op jit(solution)/shard_map/chunk0/ppermute | solution.py:28
  110.5 4.0 collective-permute-start.37
  114.6 3.7 collective-permute-done.64
  120.9 7.1 collective-permute-done.94
  128.0 3.2 collective-permute-start.7
  135.5 4.7 collective-permute-done.7
  140.2 4.1 collective-permute-start.40
  148.2 2.6 collective-permute-start.10
  152.4 4.8 collective-permute-start.42
  159.6 2.6 collective-permute-done.10
  162.3 2.6 collective-permute-start.11
  167.6 4.2 collective-permute-start.67
  176.2 23.9 %convolution_bitcast_fusion.3 = f32[3584,256]{0,1:T(8,128)} fusion(bf16[7168,256]{1,0:T(8,128)(2,1)} %bitcast.8, bf16[3584,7168]{1,0:T(8,128)(2,1)} %param.2), kind=kOutput, calls=%fused_computation.7 | convolution fusion | flops 13153337344 | bytes 58720256 | tf_op jit(solution)/shard_map/chunk0/dot_general | solution.py:193
  200.2 24.0 %convolution_bitcast_fusion.2 = f32[3584,256]{0,1:T(8,128)} fusion(bf16[7168,256]{1,0:T(8,128)(2,1)} %bitcast.18, bf16[3584,7168]{1,0:T(8,128)(2,1)} %param.2), kind=kOutput, calls=%fused_computation.6 | convolution fusion | flops 13153337344 | bytes 58720256 | tf_op jit(solution)/shard_map/chunk256/dot_general | solution.py:193
  224.1 5.4 reshape.41
  229.5 5.4 reshape.43
  240.0 3.5 collective-permute-start.70
  248.1 4.4 collective-permute-done.70
  252.5 4.1 collective-permute-start.100
  258.6 4.4 constant_dynamic-slice_fusion.48
  271.5 4.4 constant_dynamic-slice_fusion.35
  277.0 24.1 %convolution_bitcast_fusion.1 = f32[3584,256]{0,1:T(8,128)} fusion(bf16[7168,256]{1,0:T(8,128)(2,1)} %bitcast.28, bf16[3584,7168]{1,0:T(8,128)(2,1)} %param.2), kind=kOutput, calls=%fused_computation.5 | convolution fusion | flops 13153337344 | bytes 58720256 | tf_op jit(solution)/shard_map/chunk512/dot_general | solution.py:193
  301.1 5.3 reshape.45
  306.4 10.0 %constant_dynamic-slice_fusion.23 = (f32[1,896,256]{1,0,2:T(1,128)S(1)}, f32[1,896,256]{1,0,2:T(1,128)}, f32[1,896,256]{1,0,2:T(1,128)}, f32[1,896,256]{1,0,2:T(1,128)}) fusion(f32[4,896,256]{1,0,2:T(4,128)} %reshape.45, s32[]{:T(128)S(6)} %select_n.578, s32[]{:T(128)S(6)} %select_n.584, s32[]{:T(128)S(6)} %select_n.582, s32[]{:T(128)S(6)} %select_n.580), kind=kLoop, calls=%fused_computation.262 | loop fusion | bytes 7340048 | tf_op jit(solution)/shard_map/chunk512/jit(dynamic_index_in_dim)/dynamic_slice | solution.py:56
  318.1 24.1 %convolution_bitcast_fusion = f32[3584,256]{0,1:T(8,128)} fusion(bf16[7168,256]{1,0:T(8,128)(2,1)} %bitcast.38, bf16[3584,7168]{1,0:T(8,128)(2,1)} %param.2), kind=kOutput, calls=%fused_computation.4 | convolution fusion | flops 13153337344 | bytes 58720256 | tf_op jit(solution)/shard_map/chunk768/dot_general | solution.py:193
  342.3 5.3 reshape.47
  347.6 10.4 %constant_dynamic-slice_fusion.11 = (f32[1,896,256]{1,0,2:T(1,128)S(1)}, f32[1,896,256]{1,0,2:T(1,128)S(1)}, f32[1,896,256]{1,0,2:T(1,128)S(1)}, f32[1,896,256]{1,0,2:T(1,128)}) fusion(f32[4,896,256]{1,0,2:T(4,128)} %reshape.47, s32[]{:T(128)S(6)} %select_n.578, s32[]{:T(128)S(6)} %select_n.584, s32[]{:T(128)S(6)} %select_n.582, s32[]{:T(128)S(6)} %select_n.580), kind=kLoop, calls=%fused_computation.240 | loop fusion | bytes 7340048 | tf_op jit(solution)/shard_map/chunk768/jit(dynamic_index_in_dim)/dynamic_slice | solution.py:56
  369.0 5.7 collective-permute-done.13
  375.9 10.5 %collective-permute-done.14 = f16[912,256]{0,1:T(8,128)(2,1)S(1)} collective-permute-done((f16[912,256]{0,1:T(8,128)(2,1)S(1)}, f16[912,256]{0,1:T(8,128)(2,1)S(1)}, u32[]{:S(2)}, u32[]{:S(2)}) %collective-permute-start.14) | collective-permute-done | bytes 466976 | tf_op jit(solution)/shard_map/chunk0/ppermute | solution.py:64
  388.7 8.5 %collective-permute-done.43 = f16[912,256]{0,1:T(8,128)(2,1)S(1)} collective-permute-done((f16[912,256]{0,1:T(8,128)(2,1)S(1)}, f16[912,256]{0,1:T(8,128)(2,1)S(1)}, u32[]{:S(2)}, u32[]{:S(2)}) %collective-permute-start.43) | collective-permute-done | bytes 466976 | tf_op jit(solution)/shard_map/chunk256/ppermute | solution.py:64
  398.5 10.4 %collective-permute-done.44 = f16[912,256]{0,1:T(8,128)(2,1)S(1)} collective-permute-done((f16[912,256]{0,1:T(8,128)(2,1)S(1)}, f16[912,256]{0,1:T(8,128)(2,1)S(1)}, u32[]{:S(2)}, u32[]{:S(2)}) %collective-permute-start.44) | collective-permute-done | bytes 466976 | tf_op jit(solution)/shard_map/chunk256/ppermute | solution.py:64
  410.4 9.3 %collective-permute-done.73 = f16[912,256]{0,1:T(8,128)(2,1)S(1)} collective-permute-done((f16[912,256]{0,1:T(8,128)(2,1)S(1)}, f16[912,256]{0,1:T(8,128)(2,1)S(1)}, u32[]{:S(2)}, u32[]{:S(2)}) %collective-permute-start.73) | collective-permute-done | bytes 466976 | tf_op jit(solution)/shard_map/chunk512/ppermute | solution.py:64
  421.5 9.8 %collective-permute-done.74 = f16[912,256]{0,1:T(8,128)(2,1)S(1)} collective-permute-done((f16[912,256]{0,1:T(8,128)(2,1)S(1)}, f16[912,256]{0,1:T(8,128)(2,1)S(1)}, u32[]{:S(2)}, u32[]{:S(2)}) %collective-permute-start.74) | collective-permute-done | bytes 466976 | tf_op jit(solution)/shard_map/chunk512/ppermute | solution.py:64
  434.0 2.6 fusion.6
  439.4 2.8 collective-permute-done.103
  443.5 10.1 %collective-permute-done.104 = f16[912,256]{0,1:T(8,128)(2,1)S(1)} collective-permute-done((f16[912,256]{0,1:T(8,128)(2,1)S(1)}, f16[912,256]{0,1:T(8,128)(2,1)S(1)}, u32[]{:S(2)}, u32[]{:S(2)}) %collective-permute-start.104) | collective-permute-done | bytes 466976 | tf_op jit(solution)/shard_map/chunk768/ppermute | solution.py:64
  455.6 2.4 collective-permute-start.19
  464.8 3.4 fusion.4
  468.4 3.4 collective-permute-start.106
  491.4 8.5 %collective-permute-start.29 = (f32[128,256]{1,0:T(8,128)S(1)}, f32[128,256]{1,0:T(8,128)S(1)}, u32[]{:S(2)}, u32[]{:S(2)}) collective-permute-start(f32[128,256]{1,0:T(8,128)S(1)} %constant_dynamic-update-slice_fusion.32), channel_id=1, source_target_pairs={{0,4},{4,0},{8,12},{12,8},{16,20},{20,16},{24,28},{28,24},{1,5},{5... | collective-permute-start | bytes 393224 | tf_op jit(solution)/shard_map/chunk0/ppermute | solution.py:84
  503.3 35.1 %chunk0.1 = (f32[256,256]{1,0:T(8,128)S(1)}, f32[256,256]{1,0:T(8,128)S(1)}) custom-call(f32[256,256]{1,0:T(8,128)S(1)} %constant_dynamic-update-slice_fusion.30.gram_ref), custom_call_target="tpu_custom_call" | custom-call | flops 20000000000 | bytes 4000000 | tf_op jit(solution)/shard_map/chunk0/pallas_call | solution.py:171
  546.5 3.3 collective-permute-start.59
  562.7 4.2 collective-permute-done.86
  567.7 5.1 collective-permute-done.87
  572.8 3.4 collective-permute-done.88
  576.3 8.1 %collective-permute-start.89 = (f32[384,256]{1,0:T(8,128)S(1)}, f32[384,256]{1,0:T(8,128)S(1)}, u32[]{:S(2)}, u32[]{:S(2)}) collective-permute-start(f32[384,256]{1,0:T(8,128)S(1)} %constant_dynamic-update-slice_fusion.12), channel_id=1, source_target_pairs={{0,4},{4,0},{8,12},{12,8},{16,20},{20,16},{24,28},{28,24},{1,5},{5... | collective-permute-start | bytes 1179656 | tf_op jit(solution)/shard_map/chunk512/ppermute | solution.py:84
  588.9 37.2 %chunk256.1 = (f32[512,256]{1,0:T(8,128)S(1)}, f32[256,512]{1,0:T(8,128)S(1)}) custom-call(f32[512,256]{1,0:T(8,128)S(1)} %constant_dynamic-update-slice_fusion.20.gram_ref, f32[256,256]{1,0:T(8,128)S(1)} %get-tuple-element.10.refs_0_), custom_call_target="tpu_custom_call" | custom-call | flops 20000000000 | bytes 4000000 | tf_op jit(solution)/shard_map/chunk256/pallas_call | solution.py:171
  637.7 3.4 collective-permute-done.117
  642.8 39.1 %chunk512.1 = (f32[768,256]{1,0:T(8,128)S(1)}, f32[256,768]{1,0:T(8,128)S(1)}) custom-call(f32[768,256]{1,0:T(8,128)S(1)} %constant_dynamic-update-slice_fusion.10.gram_ref, f32[512,512]{1,0:T(8,128)S(1)} %select_maximum_fusion.3.refs_0_), custom_call_target="tpu_custom_call" | custom-call | flops 20000000000 | bytes 4000000 | tf_op jit(solution)/shard_map/chunk512/pallas_call | solution.py:171
  683.7 44.0 %chunk768.1 = (f32[1024,256]{1,0:T(8,128)S(1)}, f32[256,1024]{1,0:T(8,128)S(1)}) custom-call(f32[1024,256]{1,0:T(8,128)S(1)} %constant_dynamic-update-slice_fusion.gram_ref, f32[768,768]{1,0:T(8,128)S(1)} %select_maximum_fusion.2.refs_0_), custom_call_target="tpu_custom_call" | custom-call | flops 20000000000 | bytes 4000000 | tf_op jit(solution)/shard_map/chunk768/pallas_call | solution.py:171
  731.7 5.0 copy.22
  736.7 2.6 fusion
  (422 shorter events, 182.7 us)
Async XLA Ops:
  3.1 18.1 %collective-permute-start.30 = (bf16[896,256]{1,0:T(8,128)(2,1)}, bf16[896,256]{1,0:T(8,128)(2,1)}, u32[]{:S(2)}, u32[]{:S(2)}) collective-permute-start(bf16[896,256]{1,0:T(8,128)(2,1)} %get-tuple-element.73), channel_id=1, source_target_pairs={{0,4},{4,0},{8,12},{12,8},{16,20},{20,16},{24,28},{28,24},{1,5},{5... | collective-permute-start | bytes 1376264 | tf_op jit(solution)/shard_map/chunk256/ppermute | solution.py:34
  3.2 21.2 %collective-permute-start.32 = (bf16[896,256]{1,0:T(8,128)(2,1)}, bf16[896,256]{1,0:T(8,128)(2,1)}, u32[]{:S(2)}, u32[]{:S(2)}) collective-permute-start(bf16[896,256]{1,0:T(8,128)(2,1)} %get-tuple-element.73), channel_id=1, source_target_pairs={{8,0},{12,4},{16,8},{20,12},{24,16},{28,20},{9,1},{13,5},{17,9},{2... | collective-permute-start | bytes 1376264 | tf_op jit(solution)/shard_map/chunk256/ppermute | solution.py:28
  4.5 21.2 %collective-permute-start.31 = (bf16[896,256]{1,0:T(8,128)(2,1)}, bf16[896,256]{1,0:T(8,128)(2,1)}, u32[]{:S(2)}, u32[]{:S(2)}) collective-permute-start(bf16[896,256]{1,0:T(8,128)(2,1)} %get-tuple-element.73), channel_id=1, source_target_pairs={{0,8},{4,12},{8,16},{12,20},{16,24},{20,28},{1,9},{5,13},{9,17},{1... | collective-permute-start | bytes 1376264 | tf_op jit(solution)/shard_map/chunk256/ppermute | solution.py:27
  10.5 18.3 %collective-permute-start = (bf16[896,256]{1,0:T(8,128)(2,1)S(1)}, bf16[896,256]{1,0:T(8,128)(2,1)}, u32[]{:S(2)}, u32[]{:S(2)}) collective-permute-start(bf16[896,256]{1,0:T(8,128)(2,1)S(1)} %get-tuple-element.72), channel_id=1, source_target_pairs={{0,4},{4,0},{8,12},{12,8},{16,20},{20,16},{24,28},{28,24},{1,5},{5... | collective-permute-start | bytes 1376264 | tf_op jit(solution)/shard_map/chunk0/ppermute | solution.py:34
  10.8 18.3 %collective-permute-start.2 = (bf16[896,256]{1,0:T(8,128)(2,1)S(1)}, bf16[896,256]{1,0:T(8,128)(2,1)}, u32[]{:S(2)}, u32[]{:S(2)}) collective-permute-start(bf16[896,256]{1,0:T(8,128)(2,1)S(1)} %get-tuple-element.72), channel_id=1, source_target_pairs={{8,0},{12,4},{16,8},{20,12},{24,16},{28,20},{9,1},{13,5},{17,9},{2... | collective-permute-start | bytes 1376264 | tf_op jit(solution)/shard_map/chunk0/ppermute | solution.py:28
  24.4 15.3 %collective-permute-start.62 = (bf16[896,256]{1,0:T(8,128)(2,1)S(1)}, bf16[896,256]{1,0:T(8,128)(2,1)}, u32[]{:S(2)}, u32[]{:S(2)}) collective-permute-start(bf16[896,256]{1,0:T(8,128)(2,1)S(1)} %get-tuple-element.75), channel_id=1, source_target_pairs={{8,0},{12,4},{16,8},{20,12},{24,16},{28,20},{9,1},{13,5},{17,9},{2... | collective-permute-start | bytes 1376264 | tf_op jit(solution)/shard_map/chunk512/ppermute | solution.py:28
  25.7 23.7 %collective-permute-start.33 = (bf16[896,256]{1,0:T(8,128)(2,1)}, bf16[896,256]{1,0:T(8,128)(2,1)S(1)}, u32[]{:S(2)}, u32[]{:S(2)}) collective-permute-start(bf16[896,256]{1,0:T(8,128)(2,1)} %collective-permute-done.32), channel_id=1, source_target_pairs={{8,0},{12,4},{16,8},{20,12},{24,16},{28,20},{9,1},{13,5},{17,9},{2... | collective-permute-start | bytes 1376264 | tf_op jit(solution)/shard_map/chunk256/ppermute | solution.py:28
  28.8 22.6 %collective-permute-start.90 = (bf16[896,256]{1,0:T(8,128)(2,1)S(1)}, bf16[896,256]{1,0:T(8,128)(2,1)S(1)}, u32[]{:S(2)}, u32[]{:S(2)}) collective-permute-start(bf16[896,256]{1,0:T(8,128)(2,1)S(1)} %get-tuple-element.74), channel_id=1, source_target_pairs={{0,4},{4,0},{8,12},{12,8},{16,20},{20,16},{24,28},{28,24},{1,5},{5... | collective-permute-start | bytes 1376264 | tf_op jit(solution)/shard_map/chunk768/ppermute | solution.py:34
  29.1 30.2 %collective-permute-start.92 = (bf16[896,256]{1,0:T(8,128)(2,1)S(1)}, bf16[896,256]{1,0:T(8,128)(2,1)}, u32[]{:S(2)}, u32[]{:S(2)}) collective-permute-start(bf16[896,256]{1,0:T(8,128)(2,1)S(1)} %get-tuple-element.74), channel_id=1, source_target_pairs={{8,0},{12,4},{16,8},{20,12},{24,16},{28,20},{9,1},{13,5},{17,9},{2... | collective-permute-start | bytes 1376264 | tf_op jit(solution)/shard_map/chunk768/ppermute | solution.py:28
  30.4 38.7 %collective-permute-start.3 = (bf16[896,256]{1,0:T(8,128)(2,1)}, bf16[896,256]{1,0:T(8,128)(2,1)S(1)}, u32[]{:S(2)}, u32[]{:S(2)}) collective-permute-start(bf16[896,256]{1,0:T(8,128)(2,1)} %collective-permute-done.2), channel_id=1, source_target_pairs={{8,0},{12,4},{16,8},{20,12},{24,16},{28,20},{9,1},{13,5},{17,9},{2... | collective-permute-start | bytes 1376264 | tf_op jit(solution)/shard_map/chunk0/ppermute | solution.py:28
  39.6 39.2 %collective-permute-start.63 = (bf16[896,256]{1,0:T(8,128)(2,1)}, bf16[896,256]{1,0:T(8,128)(2,1)S(1)}, u32[]{:S(2)}, u32[]{:S(2)}) collective-permute-start(bf16[896,256]{1,0:T(8,128)(2,1)} %collective-permute-done.62), channel_id=1, source_target_pairs={{8,0},{12,4},{16,8},{20,12},{24,16},{28,20},{9,1},{13,5},{17,9},{2... | collective-permute-start | bytes 1376264 | tf_op jit(solution)/shard_map/chunk512/ppermute | solution.py:28
  49.4 39.3 %collective-permute-start.34 = (bf16[896,256]{1,0:T(8,128)(2,1)S(1)}, bf16[896,256]{1,0:T(8,128)(2,1)S(1)}, u32[]{:S(2)}, u32[]{:S(2)}) collective-permute-start(bf16[896,256]{1,0:T(8,128)(2,1)S(1)} %collective-permute-done.33), channel_id=1, source_target_pairs={{8,0},{12,4},{16,8},{20,12},{24,16},{28,20},{9,1},{13,5},{17,9},{2... | collective-permute-start | bytes 1376264 | tf_op jit(solution)/shard_map/chunk256/ppermute | solution.py:28
  51.5 39.4 %collective-permute-start.1 = (bf16[896,256]{1,0:T(8,128)(2,1)S(1)}, bf16[896,256]{1,0:T(8,128)(2,1)S(1)}, u32[]{:S(2)}, u32[]{:S(2)}) collective-permute-start(bf16[896,256]{1,0:T(8,128)(2,1)S(1)} %get-tuple-element.72), channel_id=1, source_target_pairs={{0,8},{4,12},{8,16},{12,20},{16,24},{20,28},{1,9},{5,13},{9,17},{1... | collective-permute-start | bytes 1376264 | tf_op jit(solution)/shard_map/chunk0/ppermute | solution.py:27
  59.3 39.2 %collective-permute-start.93 = (bf16[896,256]{1,0:T(8,128)(2,1)}, bf16[896,256]{1,0:T(8,128)(2,1)S(1)}, u32[]{:S(2)}, u32[]{:S(2)}) collective-permute-start(bf16[896,256]{1,0:T(8,128)(2,1)} %collective-permute-done.92), channel_id=1, source_target_pairs={{8,0},{12,4},{16,8},{20,12},{24,16},{28,20},{9,1},{13,5},{17,9},{2... | collective-permute-start | bytes 1376264 | tf_op jit(solution)/shard_map/chunk768/ppermute | solution.py:28
  69.0 39.3 %collective-permute-start.4 = (bf16[896,256]{1,0:T(8,128)(2,1)S(1)}, bf16[896,256]{1,0:T(8,128)(2,1)S(1)}, u32[]{:S(2)}, u32[]{:S(2)}) collective-permute-start(bf16[896,256]{1,0:T(8,128)(2,1)S(1)} %collective-permute-done.3), channel_id=1, source_target_pairs={{8,0},{12,4},{16,8},{20,12},{24,16},{28,20},{9,1},{13,5},{17,9},{2... | collective-permute-start | bytes 1376264 | tf_op jit(solution)/shard_map/chunk0/ppermute | solution.py:28
  78.9 31.7 %collective-permute-start.61 = (bf16[896,256]{1,0:T(8,128)(2,1)S(1)}, bf16[896,256]{1,0:T(8,128)(2,1)S(1)}, u32[]{:S(2)}, u32[]{:S(2)}) collective-permute-start(bf16[896,256]{1,0:T(8,128)(2,1)S(1)} %get-tuple-element.75), channel_id=1, source_target_pairs={{0,8},{4,12},{8,16},{12,20},{16,24},{20,28},{1,9},{5,13},{9,17},{1... | collective-permute-start | bytes 1376264 | tf_op jit(solution)/shard_map/chunk512/ppermute | solution.py:27
  88.7 29.6 %collective-permute-start.64 = (bf16[896,256]{1,0:T(8,128)(2,1)S(1)}, bf16[896,256]{1,0:T(8,128)(2,1)}, u32[]{:S(2)}, u32[]{:S(2)}) collective-permute-start(bf16[896,256]{1,0:T(8,128)(2,1)S(1)} %collective-permute-done.63), channel_id=1, source_target_pairs={{8,0},{12,4},{16,8},{20,12},{24,16},{28,20},{9,1},{13,5},{17,9},{2... | collective-permute-start | bytes 1376264 | tf_op jit(solution)/shard_map/chunk512/ppermute | solution.py:28
  90.9 30.1 %collective-permute-start.91 = (bf16[896,256]{1,0:T(8,128)(2,1)S(1)}, bf16[896,256]{1,0:T(8,128)(2,1)S(1)}, u32[]{:S(2)}, u32[]{:S(2)}) collective-permute-start(bf16[896,256]{1,0:T(8,128)(2,1)S(1)} %get-tuple-element.74), channel_id=1, source_target_pairs={{0,8},{4,12},{8,16},{12,20},{16,24},{20,28},{1,9},{5,13},{9,17},{1... | collective-permute-start | bytes 1376264 | tf_op jit(solution)/shard_map/chunk768/ppermute | solution.py:27
  98.5 33.6 %collective-permute-start.35 = (bf16[896,256]{1,0:T(8,128)(2,1)}, bf16[896,256]{1,0:T(8,128)(2,1)S(1)}, u32[]{:S(2)}, u32[]{:S(2)}) collective-permute-start(bf16[896,256]{1,0:T(8,128)(2,1)} %collective-permute-done.31), channel_id=1, source_target_pairs={{0,4},{4,0},{8,12},{12,8},{16,20},{20,16},{24,28},{28,24},{1,5},{5... | collective-permute-start | bytes 1376264 | tf_op jit(solution)/shard_map/chunk256/ppermute | solution.py:37
  108.3 19.7 %collective-permute-start.94 = (bf16[896,256]{1,0:T(8,128)(2,1)S(1)}, bf16[896,256]{1,0:T(8,128)(2,1)S(1)}, u32[]{:S(2)}, u32[]{:S(2)}) collective-permute-start(bf16[896,256]{1,0:T(8,128)(2,1)S(1)} %collective-permute-done.93), channel_id=1, source_target_pairs={{8,0},{12,4},{16,8},{20,12},{24,16},{28,20},{9,1},{13,5},{17,9},{2... | collective-permute-start | bytes 1376264 | tf_op jit(solution)/shard_map/chunk768/ppermute | solution.py:28
  110.5 22.6 %collective-permute-start.37 = (bf16[896,256]{1,0:T(8,128)(2,1)}, bf16[896,256]{1,0:T(8,128)(2,1)S(1)}, u32[]{:S(2)}, u32[]{:S(2)}) collective-permute-start(bf16[896,256]{1,0:T(8,128)(2,1)} %collective-permute-done.31), channel_id=1, source_target_pairs={{0,8},{4,12},{8,16},{12,20},{16,24},{20,28},{1,9},{5,13},{9,17},{1... | collective-permute-start | bytes 1376264 | tf_op jit(solution)/shard_map/chunk256/ppermute | solution.py:27
  118.3 14.9 %collective-permute-start.36 = (bf16[896,256]{1,0:T(8,128)(2,1)S(1)}, bf16[896,256]{1,0:T(8,128)(2,1)S(1)}, u32[]{:S(2)}, u32[]{:S(2)}) collective-permute-start(bf16[896,256]{1,0:T(8,128)(2,1)S(1)} %collective-permute-done.34), channel_id=1, source_target_pairs={{0,4},{4,0},{8,12},{12,8},{16,20},{20,16},{24,28},{28,24},{1,5},{5... | collective-permute-start | bytes 1376264 | tf_op jit(solution)/shard_map/chunk256/ppermute | solution.py:38
  120.9 14.5 %collective-permute-start.5 = (bf16[896,256]{1,0:T(8,128)(2,1)S(1)}, bf16[896,256]{1,0:T(8,128)(2,1)S(1)}, u32[]{:S(2)}, u32[]{:S(2)}) collective-permute-start(bf16[896,256]{1,0:T(8,128)(2,1)S(1)} %collective-permute-done.1), channel_id=1, source_target_pairs={{0,4},{4,0},{8,12},{12,8},{16,20},{20,16},{24,28},{28,24},{1,5},{5... | collective-permute-start | bytes 1376264 | tf_op jit(solution)/shard_map/chunk0/ppermute | solution.py:37
  132.1 35.6 %collective-permute-start.12 = (bf16[896,256]{1,0:T(8,128)(2,1)}, bf16[896,256]{1,0:T(8,128)(2,1)S(1)}, u32[]{:S(2)}, u32[]{:S(2)}) collective-permute-start(bf16[896,256]{1,0:T(8,128)(2,1)} %collective-permute-done.2), channel_id=1, source_target_pairs={{0,4},{4,0},{8,12},{12,8},{16,20},{20,16},{24,28},{28,24},{1,5},{5... | collective-permute-start | bytes 1376264 | tf_op jit(solution)/shard_map/chunk0/ppermute | solution.py:38
  133.1 15.0 %collective-permute-start.38 = (bf16[896,256]{1,0:T(8,128)(2,1)S(1)}, bf16[896,256]{1,0:T(8,128)(2,1)S(1)}, u32[]{:S(2)}, u32[]{:S(2)}) collective-permute-start(bf16[896,256]{1,0:T(8,128)(2,1)S(1)} %collective-permute-done.37), channel_id=1, source_target_pairs={{0,4},{4,0},{8,12},{12,8},{16,20},{20,16},{24,28},{28,24},{1,5},{5... | collective-permute-start | bytes 1376264 | tf_op jit(solution)/shard_map/chunk256/ppermute | solution.py:37
  144.3 14.8 %collective-permute-start.8 = (bf16[896,256]{1,0:T(8,128)(2,1)S(1)}, bf16[896,256]{1,0:T(8,128)(2,1)S(1)}, u32[]{:S(2)}, u32[]{:S(2)}) collective-permute-start(bf16[896,256]{1,0:T(8,128)(2,1)S(1)} %collective-permute-done.7), channel_id=1, source_target_pairs={{0,4},{4,0},{8,12},{12,8},{16,20},{20,16},{24,28},{28,24},{1,5},{5... | collective-permute-start | bytes 1376264 | tf_op jit(solution)/shard_map/chunk0/ppermute | solution.py:37
  152.4 19.4 %collective-permute-start.42 = (bf16[896,256]{1,0:T(8,128)(2,1)}, bf16[896,256]{1,0:T(8,128)(2,1)S(1)}, u32[]{:S(2)}, u32[]{:S(2)}) collective-permute-start(bf16[896,256]{1,0:T(8,128)(2,1)} %collective-permute-done.32), channel_id=1, source_target_pairs={{0,4},{4,0},{8,12},{12,8},{16,20},{20,16},{24,28},{28,24},{1,5},{5... | collective-permute-start | bytes 1376264 | tf_op jit(solution)/shard_map/chunk256/ppermute | solution.py:38
  159.1 75.7 %collective-permute-start.65 = (bf16[896,256]{1,0:T(8,128)(2,1)S(1)}, bf16[896,256]{1,0:T(8,128)(2,1)}, u32[]{:S(2)}, u32[]{:S(2)}) collective-permute-start(bf16[896,256]{1,0:T(8,128)(2,1)S(1)} %collective-permute-done.61), channel_id=1, source_target_pairs={{0,4},{4,0},{8,12},{12,8},{16,20},{20,16},{24,28},{28,24},{1,5},{5... | collective-permute-start | bytes 1376264 | tf_op jit(solution)/shard_map/chunk512/ppermute | solution.py:37
  159.2 15.3 %collective-permute-start.41 = (bf16[896,256]{1,0:T(8,128)(2,1)S(1)}, bf16[896,256]{1,0:T(8,128)(2,1)S(1)}, u32[]{:S(2)}, u32[]{:S(2)}) collective-permute-start(bf16[896,256]{1,0:T(8,128)(2,1)S(1)} %collective-permute-done.40), channel_id=1, source_target_pairs={{0,4},{4,0},{8,12},{12,8},{16,20},{20,16},{24,28},{28,24},{1,5},{5... | collective-permute-start | bytes 1376264 | tf_op jit(solution)/shard_map/chunk256/ppermute | solution.py:37
  167.6 69.9 %collective-permute-start.67 = (bf16[896,256]{1,0:T(8,128)(2,1)S(1)}, bf16[896,256]{1,0:T(8,128)(2,1)S(1)}, u32[]{:S(2)}, u32[]{:S(2)}) collective-permute-start(bf16[896,256]{1,0:T(8,128)(2,1)S(1)} %collective-permute-done.61), channel_id=1, source_target_pairs={{0,8},{4,12},{8,16},{12,20},{16,24},{20,28},{1,9},{5,13},{9,17},{1... | collective-permute-start | bytes 1376264 | tf_op jit(solution)/shard_map/chunk512/ppermute | solution.py:27
  171.8 66.8 %collective-permute-start.95 = (bf16[896,256]{1,0:T(8,128)(2,1)S(1)}, bf16[896,256]{1,0:T(8,128)(2,1)}, u32[]{:S(2)}, u32[]{:S(2)}) collective-permute-start(bf16[896,256]{1,0:T(8,128)(2,1)S(1)} %collective-permute-done.91), channel_id=1, source_target_pairs={{0,4},{4,0},{8,12},{12,8},{16,20},{20,16},{24,28},{28,24},{1,5},{5... | collective-permute-start | bytes 1376264 | tf_op jit(solution)/shard_map/chunk768/ppermute | solution.py:37
  172.1 67.8 %collective-permute-start.97 = (bf16[896,256]{1,0:T(8,128)(2,1)S(1)}, bf16[896,256]{1,0:T(8,128)(2,1)S(1)}, u32[]{:S(2)}, u32[]{:S(2)}) collective-permute-start(bf16[896,256]{1,0:T(8,128)(2,1)S(1)} %collective-permute-done.91), channel_id=1, source_target_pairs={{0,8},{4,12},{8,16},{12,20},{16,24},{20,28},{1,9},{5,13},{9,17},{1... | collective-permute-start | bytes 1376264 | tf_op jit(solution)/shard_map/chunk768/ppermute | solution.py:27
  174.4 60.5 %collective-permute-start.66 = (bf16[896,256]{1,0:T(8,128)(2,1)}, bf16[896,256]{1,0:T(8,128)(2,1)}, u32[]{:S(2)}, u32[]{:S(2)}) collective-permute-start(bf16[896,256]{1,0:T(8,128)(2,1)} %collective-permute-done.64), channel_id=1, source_target_pairs={{0,4},{4,0},{8,12},{12,8},{16,20},{20,16},{24,28},{28,24},{1,5},{5... | collective-permute-start | bytes 1376264 | tf_op jit(solution)/shard_map/chunk512/ppermute | solution.py:38
  234.9 41.0 %collective-permute-start.102 = (bf16[896,256]{1,0:T(8,128)(2,1)}, bf16[896,256]{1,0:T(8,128)(2,1)S(1)}, u32[]{:S(2)}, u32[]{:S(2)}) collective-permute-start(bf16[896,256]{1,0:T(8,128)(2,1)} %collective-permute-done.92), channel_id=1, source_target_pairs={{0,4},{4,0},{8,12},{12,8},{16,20},{20,16},{24,28},{28,24},{1,5},{5... | collective-permute-start | bytes 1376264 | tf_op jit(solution)/shard_map/chunk768/ppermute | solution.py:38
  237.5 38.3 %collective-permute-start.72 = (bf16[896,256]{1,0:T(8,128)(2,1)}, bf16[896,256]{1,0:T(8,128)(2,1)S(1)}, u32[]{:S(2)}, u32[]{:S(2)}) collective-permute-start(bf16[896,256]{1,0:T(8,128)(2,1)} %collective-permute-done.62), channel_id=1, source_target_pairs={{0,4},{4,0},{8,12},{12,8},{16,20},{20,16},{24,28},{28,24},{1,5},{5... | collective-permute-start | bytes 1376264 | tf_op jit(solution)/shard_map/chunk512/ppermute | solution.py:38
  245.3 17.6 %collective-permute-start.98 = (bf16[896,256]{1,0:T(8,128)(2,1)S(1)}, bf16[896,256]{1,0:T(8,128)(2,1)}, u32[]{:S(2)}, u32[]{:S(2)}) collective-permute-start(bf16[896,256]{1,0:T(8,128)(2,1)S(1)} %collective-permute-done.97), channel_id=1, source_target_pairs={{0,4},{4,0},{8,12},{12,8},{16,20},{20,16},{24,28},{28,24},{1,5},{5... | collective-permute-start | bytes 1376264 | tf_op jit(solution)/shard_map/chunk768/ppermute | solution.py:37
  246.1 21.2 %collective-permute-start.99 = (bf16[896,256]{1,0:T(8,128)(2,1)S(1)}, bf16[896,256]{1,0:T(8,128)(2,1)S(1)}, u32[]{:S(2)}, u32[]{:S(2)}) collective-permute-start(bf16[896,256]{1,0:T(8,128)(2,1)S(1)} %collective-permute-done.93), channel_id=1, source_target_pairs={{0,4},{4,0},{8,12},{12,8},{16,20},{20,16},{24,28},{28,24},{1,5},{5... | collective-permute-start | bytes 1376264 | tf_op jit(solution)/shard_map/chunk768/ppermute | solution.py:38
  360.1 14.6 %collective-permute-start.13 = (f16[912,256]{0,1:T(8,128)(2,1)S(1)}, f16[912,256]{0,1:T(8,128)(2,1)S(1)}, u32[]{:S(2)}, u32[]{:S(2)}) collective-permute-start(f16[912,256]{0,1:T(8,128)(2,1)S(1)} %pad_maximum_fusion.10), channel_id=1, source_target_pairs={{0,1},{1,2},{2,3},{3,0},{4,5},{5,6},{6,7},{7,4},{8,9},{9,10},{10,1... | collective-permute-start | bytes 1400840 | tf_op jit(solution)/shard_map/chunk0/ppermute | solution.py:64
  361.8 24.7 %collective-permute-start.14 = (f16[912,256]{0,1:T(8,128)(2,1)S(1)}, f16[912,256]{0,1:T(8,128)(2,1)S(1)}, u32[]{:S(2)}, u32[]{:S(2)}) collective-permute-start(f16[912,256]{0,1:T(8,128)(2,1)S(1)} %pad_maximum_fusion.11), channel_id=1, source_target_pairs={{0,2},{1,3},{2,0},{3,1},{4,6},{5,7},{6,4},{7,5},{8,10},{9,11},{10,... | collective-permute-start | bytes 1400840 | tf_op jit(solution)/shard_map/chunk0/ppermute | solution.py:64
  363.5 23.8 %collective-permute-start.15 = (f16[912,256]{0,1:T(8,128)(2,1)S(1)}, f16[912,256]{0,1:T(8,128)(2,1)S(1)}, u32[]{:S(2)}, u32[]{:S(2)}) collective-permute-start(f16[912,256]{0,1:T(8,128)(2,1)S(1)} %pad_maximum_fusion.12), channel_id=1, source_target_pairs={{0,3},{1,0},{2,1},{3,2},{4,7},{5,4},{6,5},{7,6},{8,11},{9,8},{10,9... | collective-permute-start | bytes 1400840 | tf_op jit(solution)/shard_map/chunk0/ppermute | solution.py:64
  365.1 32.1 %collective-permute-start.43 = (f16[912,256]{0,1:T(8,128)(2,1)S(1)}, f16[912,256]{0,1:T(8,128)(2,1)S(1)}, u32[]{:S(2)}, u32[]{:S(2)}) collective-permute-start(f16[912,256]{0,1:T(8,128)(2,1)S(1)} %pad_maximum_fusion.13), channel_id=1, source_target_pairs={{0,1},{1,2},{2,3},{3,0},{4,5},{5,6},{6,7},{7,4},{8,9},{9,10},{10,1... | collective-permute-start | bytes 1400840 | tf_op jit(solution)/shard_map/chunk256/ppermute | solution.py:64
  366.3 42.6 %collective-permute-start.44 = (f16[912,256]{0,1:T(8,128)(2,1)S(1)}, f16[912,256]{0,1:T(8,128)(2,1)S(1)}, u32[]{:S(2)}, u32[]{:S(2)}) collective-permute-start(f16[912,256]{0,1:T(8,128)(2,1)S(1)} %pad_maximum_fusion.14), channel_id=1, source_target_pairs={{0,2},{1,3},{2,0},{3,1},{4,6},{5,7},{6,4},{7,5},{8,10},{9,11},{10,... | collective-permute-start | bytes 1400840 | tf_op jit(solution)/shard_map/chunk256/ppermute | solution.py:64
  374.7 34.3 %collective-permute-start.45 = (f16[912,256]{0,1:T(8,128)(2,1)S(1)}, f16[912,256]{0,1:T(8,128)(2,1)S(1)}, u32[]{:S(2)}, u32[]{:S(2)}) collective-permute-start(f16[912,256]{0,1:T(8,128)(2,1)S(1)} %pad_maximum_fusion.15), channel_id=1, source_target_pairs={{0,3},{1,0},{2,1},{3,2},{4,7},{5,4},{6,5},{7,6},{8,11},{9,8},{10,9... | collective-permute-start | bytes 1400840 | tf_op jit(solution)/shard_map/chunk256/ppermute | solution.py:64
  386.4 33.3 %collective-permute-start.73 = (f16[912,256]{0,1:T(8,128)(2,1)S(1)}, f16[912,256]{0,1:T(8,128)(2,1)S(1)}, u32[]{:S(2)}, u32[]{:S(2)}) collective-permute-start(f16[912,256]{0,1:T(8,128)(2,1)S(1)} %pad_maximum_fusion.16), channel_id=1, source_target_pairs={{0,1},{1,2},{2,3},{3,0},{4,5},{5,6},{6,7},{7,4},{8,9},{9,10},{10,1... | collective-permute-start | bytes 1400840 | tf_op jit(solution)/shard_map/chunk512/ppermute | solution.py:64
  387.3 44.0 %collective-permute-start.74 = (f16[912,256]{0,1:T(8,128)(2,1)S(1)}, f16[912,256]{0,1:T(8,128)(2,1)S(1)}, u32[]{:S(2)}, u32[]{:S(2)}) collective-permute-start(f16[912,256]{0,1:T(8,128)(2,1)S(1)} %pad_maximum_fusion.17), channel_id=1, source_target_pairs={{0,2},{1,3},{2,0},{3,1},{4,6},{5,7},{6,4},{7,5},{8,10},{9,11},{10,... | collective-permute-start | bytes 1400840 | tf_op jit(solution)/shard_map/chunk512/ppermute | solution.py:64
  397.2 34.7 %collective-permute-start.75 = (f16[912,256]{0,1:T(8,128)(2,1)S(1)}, f16[912,256]{0,1:T(8,128)(2,1)S(1)}, u32[]{:S(2)}, u32[]{:S(2)}) collective-permute-start(f16[912,256]{0,1:T(8,128)(2,1)S(1)} %pad_maximum_fusion.18), channel_id=1, source_target_pairs={{0,3},{1,0},{2,1},{3,2},{4,7},{5,4},{6,5},{7,6},{8,11},{9,8},{10,9... | collective-permute-start | bytes 1400840 | tf_op jit(solution)/shard_map/chunk512/ppermute | solution.py:64
  408.9 33.3 %collective-permute-start.103 = (f16[912,256]{0,1:T(8,128)(2,1)S(1)}, f16[912,256]{0,1:T(8,128)(2,1)S(1)}, u32[]{:S(2)}, u32[]{:S(2)}) collective-permute-start(f16[912,256]{0,1:T(8,128)(2,1)S(1)} %pad_maximum_fusion.19), channel_id=1, source_target_pairs={{0,1},{1,2},{2,3},{3,0},{4,5},{5,6},{6,7},{7,4},{8,9},{9,10},{10,1... | collective-permute-start | bytes 1400840 | tf_op jit(solution)/shard_map/chunk768/ppermute | solution.py:64
  409.0 44.6 %collective-permute-start.104 = (f16[912,256]{0,1:T(8,128)(2,1)S(1)}, f16[912,256]{0,1:T(8,128)(2,1)S(1)}, u32[]{:S(2)}, u32[]{:S(2)}) collective-permute-start(f16[912,256]{0,1:T(8,128)(2,1)S(1)} %pad_maximum_fusion.20), channel_id=1, source_target_pairs={{0,2},{1,3},{2,0},{3,1},{4,6},{5,7},{6,4},{7,5},{8,10},{9,11},{10,... | collective-permute-start | bytes 1400840 | tf_op jit(solution)/shard_map/chunk768/ppermute | solution.py:64
  419.7 34.2 %collective-permute-start.105 = (f16[912,256]{0,1:T(8,128)(2,1)S(1)}, f16[912,256]{0,1:T(8,128)(2,1)S(1)}, u32[]{:S(2)}, u32[]{:S(2)}) collective-permute-start(f16[912,256]{0,1:T(8,128)(2,1)S(1)} %pad_maximum_fusion.21), channel_id=1, source_target_pairs={{0,3},{1,0},{2,1},{3,2},{4,7},{5,4},{6,5},{7,6},{8,11},{9,8},{10,9... | collective-permute-start | bytes 1400840 | tf_op jit(solution)/shard_map/chunk768/ppermute | solution.py:64
  436.7 106.2 %collective-permute-start.76 = (f32[384,256]{1,0:T(8,128)S(1)}, f32[384,256]{1,0:T(8,128)S(1)}, u32[]{:S(2)}, u32[]{:S(2)}) collective-permute-start(f32[384,256]{1,0:T(8,128)S(1)} %constant_dynamic-slice_fusion.19), channel_id=1, source_target_pairs={{0,4},{4,0},{8,12},{12,8},{16,20},{20,16},{24,28},{28,24},{1,5},{5... | collective-permute-start | bytes 1179656 | tf_op jit(solution)/shard_map/chunk512/ppermute | solution.py:75
  439.3 42.6 %collective-permute-start.46 = (f32[256,256]{1,0:T(8,128)S(1)}, f32[256,256]{1,0:T(8,128)S(1)}, u32[]{:S(2)}, u32[]{:S(2)}) collective-permute-start(f32[256,256]{1,0:T(8,128)S(1)} %constant_dynamic-slice_fusion.31), channel_id=1, source_target_pairs={{0,4},{4,0},{8,12},{12,8},{16,20},{20,16},{24,28},{28,24},{1,5},{5... | collective-permute-start | bytes 786440 | tf_op jit(solution)/shard_map/chunk256/ppermute | solution.py:75
  468.4 90.2 %collective-permute-start.106 = (f32[512,256]{1,0:T(8,128)S(1)}, f32[512,256]{1,0:T(8,128)S(1)}, u32[]{:S(2)}, u32[]{:S(2)}) collective-permute-start(f32[512,256]{1,0:T(8,128)S(1)} %constant_dynamic-slice_fusion.7), channel_id=1, source_target_pairs={{0,4},{4,0},{8,12},{12,8},{16,20},{20,16},{24,28},{28,24},{1,5},{5... | collective-permute-start | bytes 1572872 | tf_op jit(solution)/shard_map/chunk768/ppermute | solution.py:75
  499.9 39.1 %collective-permute-start.53 = (f32[16,256]{1,0:T(8,128)S(1)}, f32[16,256]{1,0:T(8,128)S(1)}, u32[]{:S(2)}, u32[]{:S(2)}) collective-permute-start(f32[16,256]{1,0:T(8,128)S(1)} %get-tuple-element.51), channel_id=1, source_target_pairs={{0,8},{4,12},{8,16},{12,20},{16,24},{20,28},{24,0},{28,4},{1,9},{5... | collective-permute-start | bytes 49160 | tf_op jit(solution)/shard_map/chunk256/ppermute | solution.py:84
  500.0 39.0 %collective-permute-start.54 = (f32[16,256]{1,0:T(8,128)S(1)}, f32[16,256]{1,0:T(8,128)S(1)}, u32[]{:S(2)}, u32[]{:S(2)}) collective-permute-start(f32[16,256]{1,0:T(8,128)S(1)} %get-tuple-element.51), channel_id=1, source_target_pairs={{0,16},{4,20},{8,24},{12,28},{16,0},{20,4},{24,8},{28,12},{1,17},{... | collective-permute-start | bytes 49160 | tf_op jit(solution)/shard_map/chunk256/ppermute | solution.py:84
  500.9 38.2 %collective-permute-start.55 = (f32[16,256]{1,0:T(8,128)S(1)}, f32[16,256]{1,0:T(8,128)S(1)}, u32[]{:S(2)}, u32[]{:S(2)}) collective-permute-start(f32[16,256]{1,0:T(8,128)S(1)} %get-tuple-element.51), channel_id=1, source_target_pairs={{0,24},{4,28},{8,0},{12,4},{16,8},{20,12},{24,16},{28,20},{1,25},{... | collective-permute-start | bytes 49160 | tf_op jit(solution)/shard_map/chunk256/ppermute | solution.py:84
  546.5 42.4 %collective-permute-start.59 = (f32[256,256]{1,0:T(8,128)S(1)}, f32[256,256]{1,0:T(8,128)S(1)}, u32[]{:S(2)}, u32[]{:S(2)}) collective-permute-start(f32[256,256]{1,0:T(8,128)S(1)} %constant_dynamic-update-slice_fusion.22), channel_id=1, source_target_pairs={{0,4},{4,0},{8,12},{12,8},{16,20},{20,16},{24,28},{28,24},{1,5},{5... | collective-permute-start | bytes 786440 | tf_op jit(solution)/shard_map/chunk256/ppermute | solution.py:84
  558.8 25.7 %collective-permute-start.107 = (f32[128,256]{1,0:T(8,128)S(1)}, f32[128,256]{1,0:T(8,128)S(1)}, u32[]{:S(2)}, u32[]{:S(2)}) collective-permute-start(f32[128,256]{1,0:T(8,128)S(1)} %get-tuple-element.76), channel_id=1, source_target_pairs={{0,1},{1,2},{2,3},{3,0},{4,5},{5,6},{6,7},{7,4},{8,9},{9,10},{10,1... | collective-permute-start | bytes 393224 | tf_op jit(solution)/shard_map/chunk768/ppermute | solution.py:75
  560.1 24.4 %collective-permute-start.108 = (f32[128,256]{1,0:T(8,128)S(1)}, f32[128,256]{1,0:T(8,128)S(1)}, u32[]{:S(2)}, u32[]{:S(2)}) collective-permute-start(f32[128,256]{1,0:T(8,128)S(1)} %get-tuple-element.78), channel_id=1, source_target_pairs={{0,2},{1,3},{2,0},{3,1},{4,6},{5,7},{6,4},{7,5},{8,10},{9,11},{10,... | collective-permute-start | bytes 393224 | tf_op jit(solution)/shard_map/chunk768/ppermute | solution.py:75
  561.1 23.3 %collective-permute-start.109 = (f32[128,256]{1,0:T(8,128)S(1)}, f32[128,256]{1,0:T(8,128)S(1)}, u32[]{:S(2)}, u32[]{:S(2)}) collective-permute-start(f32[128,256]{1,0:T(8,128)S(1)} %get-tuple-element.77), channel_id=1, source_target_pairs={{0,3},{1,0},{2,1},{3,2},{4,7},{5,4},{6,5},{7,6},{8,11},{9,8},{10,9... | collective-permute-start | bytes 393224 | tf_op jit(solution)/shard_map/chunk768/ppermute | solution.py:75
  576.3 66.5 %collective-permute-start.89 = (f32[384,256]{1,0:T(8,128)S(1)}, f32[384,256]{1,0:T(8,128)S(1)}, u32[]{:S(2)}, u32[]{:S(2)}) collective-permute-start(f32[384,256]{1,0:T(8,128)S(1)} %constant_dynamic-update-slice_fusion.12), channel_id=1, source_target_pairs={{0,4},{4,0},{8,12},{12,8},{16,20},{20,16},{24,28},{28,24},{1,5},{5... | collective-permute-start | bytes 1179656 | tf_op jit(solution)/shard_map/chunk512/ppermute | solution.py:84
  584.5 41.5 %collective-permute-start.110 = (f32[32,256]{1,0:T(8,128)S(1)}, f32[32,256]{1,0:T(8,128)S(1)}, u32[]{:S(2)}, u32[]{:S(2)}) collective-permute-start(f32[32,256]{1,0:T(8,128)S(1)} %get-tuple-element.88), channel_id=1, source_target_pairs={{0,8},{4,12},{8,16},{12,20},{16,24},{20,28},{24,0},{28,4},{1,9},{5... | collective-permute-start | bytes 98312 | tf_op jit(solution)/shard_map/chunk768/ppermute | solution.py:75
  586.3 39.8 %collective-permute-start.111 = (f32[32,256]{1,0:T(8,128)S(1)}, f32[32,256]{1,0:T(8,128)S(1)}, u32[]{:S(2)}, u32[]{:S(2)}) collective-permute-start(f32[32,256]{1,0:T(8,128)S(1)} %get-tuple-element.90), channel_id=1, source_target_pairs={{0,16},{4,20},{8,24},{12,28},{16,0},{20,4},{24,8},{28,12},{1,17},{... | collective-permute-start | bytes 98312 | tf_op jit(solution)/shard_map/chunk768/ppermute | solution.py:75
  586.5 39.6 %collective-permute-start.112 = (f32[32,256]{1,0:T(8,128)S(1)}, f32[32,256]{1,0:T(8,128)S(1)}, u32[]{:S(2)}, u32[]{:S(2)}) collective-permute-start(f32[32,256]{1,0:T(8,128)S(1)} %get-tuple-element.89), channel_id=1, source_target_pairs={{0,24},{4,28},{8,0},{12,4},{16,8},{20,12},{24,16},{28,20},{1,25},{... | collective-permute-start | bytes 98312 | tf_op jit(solution)/shard_map/chunk768/ppermute | solution.py:75
  641.2 42.5 %collective-permute-start.119 = (f32[512,256]{1,0:T(8,128)S(1)}, f32[512,256]{1,0:T(8,128)S(1)}, u32[]{:S(2)}, u32[]{:S(2)}) collective-permute-start(f32[512,256]{1,0:T(8,128)S(1)} %constant_dynamic-update-slice_fusion.2), channel_id=1, source_target_pairs={{0,4},{4,0},{8,12},{12,8},{16,20},{20,16},{24,28},{28,24},{1,5},{5... | collective-permute-start | bytes 1572872 | tf_op jit(solution)/shard_map/chunk768/ppermute | solution.py:84
  (71 other events, 454.2 us)
